TPU v7x, 32 devices: a whole 2x2x4 slice. The times are simulated.
32 devices in a mesh: gx: 4 (over y, x), gy: 8 (over z, core).
Axes of the slice: x: 2, y: 2, z: 4, core: 2. Of those that a mesh axis runs over, the one named last changes fastest.
Arguments:
- rhs_base: float32 [8, 64, 1024], P(None, 'gx', 'gy'), may hold values from -12 to 12
- cond_base: float32 [8, 64, 1024], P(None, 'gx', 'gy'), may hold values from 0.1 to 1
- cap_base: float32 [8, 64, 1024], P(None, 'gx', 'gy'), may hold values from 0.02 to 0.5
- patch_rhs: float32 [512, 8, 256], P(('gx', 'gy')), may hold values from -12 to 12
- patch_cond: float32 [512, 8, 256], P(('gx', 'gy')), may hold values from 0.1 to 1
- patch_cap: float32 [512, 8, 256], P(('gx', 'gy')), may hold values from 0.02 to 0.5
- box_list: int32 [1024, 2], P(('gx', 'gy')), may hold values from -1 to 31, as said below
- patch_from: int32 [512], P(('gx', 'gy')), may hold values from 0 to 31, as said below
Outputs:
- solution_field: float32 [8, 64, 1024], P(None, 'gx', 'gy')
- patch_field: float32 [512, 8, 256], P(('gx', 'gy'))
Inputs may be any that keep to these rules, and one draw needn't show every extreme that they name: `box_list`: rows (a 8 + b) * 32 to (a 8 + b + 1) * 32 - 1 are tile (a, b)'s boxes: column 0 a footprint slot, column 1 the send row o * 4 + c for its c-th box to owner (a, o). Used entries come first, unused ones hold -1 in both columns; slots and send rows are distinct within a tile; each owner receives exactly 16 boxes in all. `patch_from`: entry (a 8 + o) * 16 + j is s * 4 + c for the box of tile (a, s) with send row o * 4 + c; the 16 entries of one device are distinct.
All inputs are finite; a program needn't handle non-finite values.
Results may differ from a plain program's by a relative error of at most 0.0001.
Values sent between devices are 32-bit elements; how exact they have to be, the bound alone decides.
A program may use at most 128 MiB of HBM per device.

v0:
```python
import functools
import jax
import jax.numpy as jnp
from jax import lax
from jax.experimental import pallas as pl
from jax.experimental.pallas import tpu as pltpu
from jax.sharding import PartitionSpec as P

SWEEPS = 12
RELAX = 0.8
F32 = jnp.float32
HALO = 4
MESH = pl.DeviceIdType.MESH


def table(rows, cols, rule):
    src = lax.broadcasted_iota(jnp.int32, (rows, cols), 0)
    dst = lax.broadcasted_iota(jnp.int32, (rows, cols), 1)
    return rule(src, dst).astype(jnp.bfloat16)


def apply_table(values, matrix):
    lead = values.shape[:-1]
    flat = values.reshape(-1, values.shape[-1])
    high = flat.astype(jnp.bfloat16)
    low = (flat - high.astype(F32)).astype(jnp.bfloat16)
    out = jnp.dot(high, matrix, preferred_element_type=F32) + jnp.dot(
        low, matrix, preferred_element_type=F32
    )
    return out.reshape(lead + (matrix.shape[1],))


def lanes(values, shift):
    return pltpu.roll(values, shift % values.shape[-1], values.ndim - 1)


def layers(values, shift):
    return pltpu.roll(values, shift % 8, values.ndim - 2)


def rows_up(values):
    return jnp.concatenate([values[1:], jnp.zeros_like(values[:1])], axis=0)


def rows_down(values):
    return jnp.concatenate([jnp.zeros_like(values[:1]), values[:-1]], axis=0)


def stencil_of(conduct, capacity, weight, mask):
    half = 0.5 * weight
    layer = lax.broadcasted_iota(jnp.int32, conduct.shape, 1)
    east = half * (conduct + rows_up(conduct))
    west = half * (conduct + rows_down(conduct))
    north = half * (conduct + lanes(conduct, -1))
    above = jnp.where(layer < 7, 0.5 * (conduct + layers(conduct, -1)), 0.0)
    diagonal = (
        capacity + east + west + north + lanes(north, 1) + above + layers(above, 1)
    )
    gain = jnp.where(mask, RELAX / diagonal, 0.0)
    return (east, west, north, above, diagonal, gain)


def around(values, stencil):
    east, west, north, above, _, _ = stencil
    return (
        east * rows_up(values)
        + west * rows_down(values)
        + north * lanes(values, -1)
        + lanes(north * values, 1)
        + above * layers(values, -1)
        + layers(above * values, 1)
    )


def smooth(values, source, stencil):
    return (1.0 - RELAX) * values + stencil[5] * (source + around(values, stencil))


def residual_of(values, source, stencil):
    return source - stencil[4] * values + around(values, stencil)


def pair_rows(values):
    count = values.shape[0] // 2
    split = values.reshape((count, 2) + values.shape[1:])
    return split[:, 0] + split[:, 1]


def repeat_rows(values):
    count = values.shape[0]
    return jnp.broadcast_to(values[:, None], (count, 2) + values.shape[1:]).reshape(
        (2 * count,) + values.shape[1:]
    )


def exchange_groups(items):
    group = lax.broadcasted_iota(jnp.int32, (8, 128), 1) // 8
    turned = [items[(-n) % 16] for n in range(16)]
    turned = [lanes(v, 8 * ((-n) % 16)) if n else v for n, v in enumerate(turned)]
    for bit in range(4):
        step = 1 << bit
        picked = (group // step) % 2 == 1
        turned = [jnp.where(picked, turned[(n - step) % 16], turned[n]) for n in range(16)]
    return [lanes(v, -8 * n) if n else v for n, v in enumerate(turned)]


def windows_into(field, out_ref):
    lane = lax.broadcasted_iota(jnp.int32, (8, 128), 1)
    for band in range(2):
        first = HALO + 8 * band
        items = [field[first + i, :, :128] for i in range(8)]
        south = jnp.zeros((8, 128), F32)
        north = jnp.zeros((8, 128), F32)
        for i in range(8):
            edge = jnp.where((lane == 0) | (lane == 127), field[first + i, :, 128:], items[i])
            south = jnp.where(lane % 8 == i, lanes(edge, i + 1), south)
            north = jnp.where(lane % 8 == i, lanes(edge, i - 8), north)
        items = items + [field[first - 1, :, :128], field[first + 8, :, :128], south, north]
        items = items + [jnp.zeros((8, 128), F32)] * 4
        for col, window in enumerate(exchange_groups(items)):
            out_ref[16 * band + col] = window


def kernel(
    n_gx, n_gy, cap_rows, tables, froms,
    rhs_ref, cond_ref, capb_ref, prhs_ref, pcond_ref, pcap_ref,
    field_ref, patch_ref,
    tile, side, from_rows, from_side, from_corner,
    slots, out1, in1, out2, in2, out3, in3, win1, win2, rest,
    coarse_k, coarse_g, column,
    send_a, recv_a, send_x, recv_x, send_k, recv_k, send_g, recv_g,
):
    a = lax.axis_index("gx")
    b = lax.axis_index("gy")
    has_up, has_down = a > 0, a < n_gx - 1
    has_left, has_right = b > 0, b < n_gy - 1
    ok_gx = {-1: has_up, 0: None, 1: has_down}
    ok_gy = {-1: has_left, 0: None, 1: has_right}

    def guarded(cond, action):
        if cond is None:
            action()
        else:
            pl.when(cond)(action)

    barrier = pltpu.get_barrier_semaphore()

    def greet(x, y):
        pl.semaphore_signal(barrier, inc=1, device_id=(x, y), device_id_type=MESH)

    for d in range(1, n_gy):
        greet(a, lax.rem(b + d, n_gy))
    for d in range(1, n_gx):
        for dy in (-1, 0, 1):
            guarded(ok_gy[dy], lambda d=d, dy=dy: greet(lax.rem(a + d, n_gx), b + dy))
    columns = 1 + has_left.astype(jnp.int32) + has_right.astype(jnp.int32)

    lane = lax.broadcasted_iota(jnp.int32, (8, 128), 1)
    own = []
    for index, ref in enumerate((cond_ref, capb_ref, rhs_ref)):
        rows = [ref[pl.ds(x, 8, stride=16), :] for x in range(16)]
        for x in range(16):
            tile[index, x] = rows[x]
        for part in range(2):
            packed = lanes(rows[8 * part], 8)
            for i in range(1, 8):
                packed = jnp.where(lane // 16 == i, lanes(rows[8 * part + i], 8 + 16 * i), packed)
            side[part, index] = packed
        own.append(jnp.stack(rows))

    pl.semaphore_wait(barrier, n_gy - 1 + (n_gx - 1) * columns)

    def start_wait(copies):
        for cond, make in copies:
            guarded(cond, lambda make=make: make().start())

    def wait_recv(copies):
        for cond, make in copies:
            guarded(cond, lambda make=make: make().wait_recv())

    def wait_send(copies):
        for cond, make in copies:
            guarded(cond, lambda make=make: make().wait_send())

    def remote(src, dst, ssem, rsem, x, y):
        return pltpu.make_async_remote_copy(
            src_ref=src, dst_ref=dst, send_sem=ssem, recv_sem=rsem,
            device_id=(x, y), device_id_type=MESH,
        )

    halo_send, halo_recv = [], []
    for dx in (-1, 0, 1):
        for dy in (-1, 0, 1):
            if dx == 0 and dy == 0:
                continue
            conds = [c for c in (ok_gx[dx], ok_gy[dy]) if c is not None]
            cond = conds[0] if len(conds) == 1 else jnp.logical_and(conds[0], conds[1])
            place = 3 * (dx + 1) + dy + 1
            back = 3 * (1 - dx) + 1 - dy

            def views(dx=dx, dy=dy):
                if dy == 0:
                    start = 0 if dx < 0 else 16 - HALO
                    return tile.at[:, pl.ds(start, HALO)], from_rows.at[(1 - dx) // 2]
                if dx == 0:
                    return side, from_side.at[(1 - dy) // 2]
                part = 0 if dx < 0 else 1
                return side.at[part], from_corner.at[(1 - dx) // 2, (1 - dy) // 2]

            def landing(dx=dx, dy=dy):
                if dy == 0:
                    return from_rows.at[(1 + dx) // 2]
                if dx == 0:
                    return from_side.at[(1 + dy) // 2]
                return from_corner.at[(1 + dx) // 2, (1 + dy) // 2]

            def out(views=views, dx=dx, dy=dy, place=place, back=back):
                src, dst = views()
                return remote(src, dst, send_a.at[place], recv_a.at[back], a + dx, b + dy)

            def arrive(landing=landing, dx=dx, dy=dy, place=place):
                return remote(landing(), landing(), send_a.at[place], recv_a.at[place], a + dx, b + dy)

            halo_send.append((cond, out))
            halo_recv.append((cond, arrive))
    start_wait(halo_send)

    def all_to_all(phase, src, dst):
        sends, recvs = [], []
        for d in range(1, n_gy):
            def out(d=d):
                to = lax.rem(b + d, n_gy)
                return remote(
                    src.at[pl.ds(to * cap_rows, cap_rows)], dst.at[pl.ds(b * cap_rows, cap_rows)],
                    send_x.at[phase, d], recv_x.at[phase, d], a, to,
                )

            def arrive(d=d):
                at = lax.rem(b + n_gy - d, n_gy)
                piece = dst.at[pl.ds(at * cap_rows, cap_rows)]
                return remote(piece, piece, send_x.at[phase, d], recv_x.at[phase, d], a, at)

            sends.append((None, out))
            recvs.append((None, arrive))
        start_wait(sends)
        mine = pl.ds(b * cap_rows, cap_rows)
        dst[mine] = src[mine]
        return sends, recvs

    def gather(buffer, ssem, rsem):
        sends, recvs = [], []
        for dy in (0, -1, 1):
            for d in range(n_gx):
                if dy == 0 and d == 0:
                    continue

                def out(d=d, dy=dy):
                    to = lax.rem(a + d, n_gx)
                    return remote(
                        buffer.at[1, a], buffer.at[1 - dy, a],
                        ssem.at[dy + 1, d], rsem.at[1 - dy, d], to, b + dy,
                    )

                def arrive(d=d, dy=dy):
                    at = lax.rem(a + n_gx - d, n_gx)
                    piece = buffer.at[dy + 1, at]
                    return remote(piece, piece, ssem.at[dy + 1, d], rsem.at[dy + 1, d], at, b + dy)

                sends.append((ok_gy[dy], out))
                recvs.append((ok_gy[dy], arrive))
        start_wait(sends)
        return sends, recvs

    to_half = table(128, 128, lambda s, d: jnp.where(s // 2 == d % 64, 0.25, 0.0))
    rim_map = table(128, 256, lambda s, d: (
        jnp.where((d < 16) & (s == 64 + d // 2), 1.0, 0.0)
        + jnp.where((d >= 240) & (s == 72 + d % 16 // 2), 1.0, 0.0)
        + jnp.where((d % 16 == 0) & (s == 80 + d // 32), 1.0, 0.0)
        + jnp.where((d % 16 == 15) & (s == 88 + d // 32), 1.0, 0.0)
    ))
    restrict_map = table(256, 128, lambda s, d: jnp.where(s // 32 * 8 + s % 16 // 2 == d, 0.25, 0.0))

    def packed_coarse(values):
        halves = apply_table(pair_rows(values), to_half)
        left = lax.broadcasted_iota(jnp.int32, (4, 8, 128), 2) < 64
        return jnp.where(left, halves[:4], halves[4:])

    coarse_k[1, a, 0] = packed_coarse(own[0])
    coarse_k[1, a, 1] = packed_coarse(own[1])

    pcond = pcond_ref[...]
    plane = lax.broadcasted_iota(jnp.int32, pcond.shape, 2)
    player = lax.broadcasted_iota(jnp.int32, pcond.shape, 1)
    p_east = jnp.where(plane < 240, 32.0 * (pcond + lanes(pcond, -16)), 0.0)
    p_north = jnp.where(plane % 16 < 15, 32.0 * (pcond + lanes(pcond, -1)), 0.0)
    p_above = jnp.where(player < 7, 0.5 * (pcond + layers(pcond, -1)), 0.0)
    outside = (
        jnp.where((plane < 16) | (plane >= 240), 64.0, 0.0)
        + jnp.where((plane % 16 == 0) | (plane % 16 == 15), 64.0, 0.0)
    )
    p_diag = (
        pcap_ref[...] + outside * pcond + p_east + lanes(p_east, 16)
        + p_north + lanes(p_north, 1) + p_above + layers(p_above, 1)
    )
    p_gain = RELAX / p_diag

    def p_around(values):
        return (
            p_east * lanes(values, -16) + lanes(p_east * values, 16)
            + p_north * lanes(values, -1) + lanes(p_north * values, 1)
            + p_above * layers(values, -1) + layers(p_above * values, 1)
        )

    wait_recv(halo_recv)
    count = 16 + 2 * HALO
    shape0 = (count, 8, 256)
    row0 = lax.broadcasted_iota(jnp.int32, shape0, 0)
    lane0 = lax.broadcasted_iota(jnp.int32, shape0, 2)
    left_i, right_i = has_left.astype(jnp.int32), has_right.astype(jnp.int32)
    up_i, down_i = has_up.astype(jnp.int32), has_down.astype(jnp.int32)
    inside0 = (
        (row0 >= HALO * (1 - up_i)) & (row0 < 16 + HALO + HALO * down_i)
        & ((lane0 < 128) | ((lane0 < 192) & (right_i > 0)) | ((lane0 >= 192) & (left_i > 0)))
    )
    last8 = lane % 16 < 8
    framed = []
    for index in range(3):
        body = jnp.concatenate([from_rows[0, index], own[index], from_rows[1, index]], axis=0)
        middle = [jnp.where(last8, from_side[0, p, index], from_side[1, p, index]) for p in range(2)]
        upper = jnp.where(last8, from_corner[0, 0, index], from_corner[0, 1, index])
        lower = jnp.where(last8, from_corner[1, 0, index], from_corner[1, 1, index])
        flank = []
        for x in range(-HALO, 16 + HALO):
            source = upper if x < 0 else lower if x >= 16 else middle[x // 8]
            flank.append(lanes(source, -(16 * (x % 8) + 8)))
        body = jnp.concatenate([body, jnp.stack(flank)], axis=2)
        framed.append(jnp.where(inside0, body, 0.0))
    stencil0 = stencil_of(framed[0], framed[1], 16.0, inside0)
    source0 = framed[2]
    u_a = smooth(stencil0[5] * source0, source0, stencil0)

    windows_into(u_a, slots)
    for r in range(32):
        out1[r] = slots[tables[r]]
    sends1, recvs1 = all_to_all(0, out1, in1)
    sends_k, recvs_k = gather(coarse_k, send_k, recv_k)
    r_0 = residual_of(u_a, source0, stencil0)[HALO:HALO + 16, :, :128]

    wait_recv(recvs1)
    for j in range(16):
        win1[j] = in1[froms[j]]
    first = win1[...]
    p_rhs = prhs_ref[...]
    p_edge = 64.0 * pcond
    p_source = p_rhs + p_edge * apply_table(first, rim_map)
    v_a = p_gain * p_source
    v_a = (1.0 - RELAX) * v_a + p_gain * (p_source + p_around(v_a))
    rest[...] = apply_table(p_source - p_diag * v_a + p_around(v_a), restrict_map)
    for r in range(32):
        out2[r] = rest[tables[64 + r]]
    sends2, recvs2 = all_to_all(1, out2, in2)

    wait_recv(recvs_k)
    rows1 = 8 * n_gx

    def spread_tiles(piece):
        left = lax.broadcasted_iota(jnp.int32, (4, 8, 128), 2) < 64
        blocks = []
        for t in range(n_gx):
            low, mid, high = piece(0, t), piece(1, t), piece(2, t)
            low_r, mid_r, high_r = lanes(low, 64), lanes(mid, 64), lanes(high, 64)
            blocks.append(jnp.concatenate([jnp.where(left, mid, high_r), low_r], axis=2))
            blocks.append(jnp.concatenate([jnp.where(left, mid_r, high), low], axis=2))
        return jnp.concatenate(blocks, axis=0)

    def inside_of(rows, width):
        lane_in = lax.broadcasted_iota(jnp.int32, (rows, 8, max(width * 4, 128)), 2)
        part = lane_in // width % 4
        return (part == 0) | ((part == 1) & (right_i > 0)) | ((part == 3) & (left_i > 0))

    halve_1 = table(256, 128, lambda s, d: jnp.where(s // 2 == d, 0.25, 0.0))
    halve_2 = to_half
    widen_3 = table(128, 128, lambda s, d: jnp.where(s == d // 2, 1.0, 0.0))
    widen_2 = table(128, 256, lambda s, d: jnp.where(s == d // 2, 1.0, 0.0))
    widen_1 = table(256, 256, lambda s, d: jnp.where(
        s == d // 2 + jnp.where(d >= 192, 128, 0), 1.0, 0.0))

    inside1 = inside_of(rows1, 64)
    k1 = jnp.where(inside1, spread_tiles(lambda s, t: coarse_k[s, t, 0]), 0.0)
    c1 = jnp.where(inside1, spread_tiles(lambda s, t: coarse_k[s, t, 1]), 0.0)
    k2, c2 = apply_table(pair_rows(k1), halve_1), apply_table(pair_rows(c1), halve_1)
    k3, c3 = apply_table(pair_rows(k2), halve_2), apply_table(pair_rows(c2), halve_2)
    stencil1 = stencil_of(k1, c1, 4.0, inside1)
    stencil2 = stencil_of(k2, c2, 1.0, inside_of(rows1 // 2, 32))
    stencil3 = stencil_of(k3, c3, 0.25, inside_of(rows1 // 4, 16))

    wait_recv(recvs2)
    pieces = []
    for band in range(2):
        items = []
        for col in range(16):
            at = tables[32 + 16 * band + col]
            flag = jnp.where(at >= 0, 1.0, 0.0).astype(F32)
            items.append(jnp.where(lane // 8 == 8, flag, in2[jnp.maximum(at, 0)]))
        placed = exchange_groups(items)
        for i in range(8):
            pieces.append(jnp.where(placed[8] > 0.5, placed[i], r_0[8 * band + i]))
    coarse_g[1, a] = packed_coarse(jnp.stack(pieces))
    sends_g, recvs_g = gather(coarse_g, send_g, recv_g)
    wait_recv(recvs_g)

    g1 = jnp.where(inside1, spread_tiles(lambda s, t: coarse_g[s, t]), 0.0)
    e1 = smooth(stencil1[5] * g1, g1, stencil1)
    g2 = apply_table(pair_rows(residual_of(e1, g1, stencil1)), halve_1)
    e2 = smooth(stencil2[5] * g2, g2, stencil2)
    g3 = apply_table(pair_rows(residual_of(e2, g2, stencil2)), halve_2)
    e3 = stencil3[5] * g3
    e3 = lax.fori_loop(0, SWEEPS - 1, lambda _, v: smooth(v, g3, stencil3), e3)
    e2 = smooth(e2 + apply_table(repeat_rows(e3), widen_3), g2, stencil2)
    e1 = smooth(e1 + apply_table(repeat_rows(e2), widen_2), g1, stencil1)
    column[pl.ds(0, 2)] = jnp.zeros((2, 8, 256), F32)
    column[pl.ds(rows1 + 2, 2)] = jnp.zeros((2, 8, 256), F32)
    column[pl.ds(2, rows1)] = e1
    near = column[pl.ds(8 * a, 12)]
    u_b = u_a + jnp.where(inside0, apply_table(repeat_rows(near), widen_1), 0.0)
    solved = smooth(u_b, source0, stencil0)

    windows_into(solved, slots)
    for r in range(32):
        out3[r] = slots[tables[r]]
    sends3, recvs3 = all_to_all(2, out3, in3)
    for x in range(16):
        field_ref[pl.ds(x, 8, stride=16), :] = solved[HALO + x, :, :128]
    grow_map = table(128, 256, lambda s, d: jnp.where(s == d // 32 * 8 + d % 16 // 2, 1.0, 0.0))
    wait_recv(recvs3)
    for j in range(16):
        win2[j] = in3[froms[j]]
    second = win2[...]
    values = v_a + apply_table(second - first, grow_map)
    p_source = p_rhs + p_edge * apply_table(second, rim_map)
    patch_ref[...] = (1.0 - RELAX) * values + p_gain * (p_source + p_around(values))

    for copies in (halo_send, sends1, sends_k, sends2, sends_g, sends3):
        wait_send(copies)


def body(n_gx, n_gy, rhs_base, cond_base, cap_base, patch_rhs, patch_cond, patch_cap, box_list, patch_from):
    rows_all = 2 * patch_rhs.shape[0]
    cap_rows = rows_all // n_gy
    ids = lax.broadcasted_iota(jnp.int32, (rows_all, 1), 0)
    slot_ids, send_rows = box_list[:, 0][None, :], box_list[:, 1][None, :]
    owned = lax.broadcasted_iota(jnp.int32, (1, patch_from.shape[0]), 1)
    tables = jnp.concatenate([
        jnp.max(jnp.where(send_rows == ids, slot_ids, 0), axis=1),
        jnp.max(jnp.where(slot_ids == ids, send_rows, -1), axis=1),
        jnp.max(jnp.where(patch_from[None, :] == ids, owned, 0), axis=1),
    ])
    vmem = pl.BlockSpec(memory_space=pltpu.VMEM)
    smem = pl.BlockSpec(memory_space=pltpu.SMEM)
    dma = pltpu.SemaphoreType.DMA
    buffer = pltpu.VMEM((32, 8, 128), F32)
    field, patches = pl.pallas_call(
        functools.partial(kernel, n_gx, n_gy, cap_rows),
        out_shape=(
            jax.ShapeDtypeStruct((128, 128), F32),
            jax.ShapeDtypeStruct(patch_rhs.shape, F32),
        ),
        in_specs=[smem, smem] + [vmem] * 6,
        out_specs=(vmem, vmem),
        scratch_shapes=[
            pltpu.VMEM((3, 16, 8, 128), F32),
            pltpu.VMEM((2, 3, 8, 128), F32),
            pltpu.VMEM((2, 3, HALO, 8, 128), F32),
            pltpu.VMEM((2, 2, 3, 8, 128), F32),
            pltpu.VMEM((2, 2, 3, 8, 128), F32),
            buffer, buffer, buffer, buffer, buffer, buffer, buffer,
            pltpu.VMEM((16, 8, 128), F32),
            pltpu.VMEM((16, 8, 128), F32),
            pltpu.VMEM((16, 8, 128), F32),
            pltpu.VMEM((3, n_gx, 2, 4, 8, 128), F32),
            pltpu.VMEM((3, n_gx, 4, 8, 128), F32),
            pltpu.VMEM((8 * n_gx + 4, 8, 256), F32),
            dma((9,)), dma((9,)),
            dma((3, n_gy)), dma((3, n_gy)),
            dma((3, n_gx)), dma((3, n_gx)),
            dma((3, n_gx)), dma((3, n_gx)),
        ],
        compiler_params=pltpu.CompilerParams(
            collective_id=0, has_side_effects=True, vmem_limit_bytes=48 * 1024 * 1024
        ),
    )(
        tables, patch_from,
        rhs_base.reshape(128, 128), cond_base.reshape(128, 128), cap_base.reshape(128, 128),
        patch_rhs, patch_cond, patch_cap,
    )
    return field.reshape(rhs_base.shape), patches


def solution(mesh):
    return jax.shard_map(
        functools.partial(body, mesh.shape["gx"], mesh.shape["gy"]),
        mesh=mesh,
        in_specs=(
            P(None, "gx", "gy"),
            P(None, "gx", "gy"),
            P(None, "gx", "gy"),
            P(("gx", "gy"), None, None),
            P(("gx", "gy"), None, None),
            P(("gx", "gy"), None, None),
            P(("gx", "gy"), None),
            P(("gx", "gy")),
        ),
        out_specs=(P(None, "gx", "gy"), P(("gx", "gy"), None, None)),
        check_vma=False,
    )
```

profile of v0, /device:TPU:0, one launch (start us, length us, event | category | flops | bytes accessed | tf_op | source)
XLA Modules:
  0.0 43.5 jit_solution(9938062627996547791)
XLA Ops:
  0.6 0.0 copy-start.6
  0.6 0.6 %copy-done.6 = s32[16]{0:T(128)S(1)} copy-done((s32[16]{0:T(128)S(1)}, s32[16]{0:T(128)}, u32[]{:S(2)}) %copy-start.6) | copy-done | bytes 88
  1.3 0.0 copy-start.7
  1.3 0.1 select_reduce_fusion.2
  1.4 0.6 %copy-done.7 = s32[32,2]{0,1:T(2,128)S(1)} copy-done((s32[32,2]{0,1:T(2,128)S(1)}, s32[32,2]{0,1:T(2,128)}, u32[]{:S(2)}) %copy-start.7) | copy-done | bytes 280
  2.0 0.1 select_reduce_fusion.1
  2.1 0.1 pad_add_fusion.tables
  2.2 0.0 copy-start
  2.2 0.9 %copy-done = f32[16,8,256]{2,1,0:T(8,128)S(1)} copy-done((f32[16,8,256]{2,1,0:T(8,128)S(1)}, f32[16,8,256]{2,1,0:T(8,128)}, u32[]{:S(2)}) %copy-start) | copy-done | bytes 131096
  3.1 0.0 copy-start.1
  3.1 0.9 %copy-done.1 = f32[16,8,256]{2,1,0:T(8,128)S(1)} copy-done((f32[16,8,256]{2,1,0:T(8,128)S(1)}, f32[16,8,256]{2,1,0:T(8,128)}, u32[]{:S(2)}) %copy-start.1) | copy-done | bytes 131096
  4.0 0.0 copy-start.2
  4.0 0.9 %copy-done.2 = f32[16,8,256]{2,1,0:T(8,128)S(1)} copy-done((f32[16,8,256]{2,1,0:T(8,128)S(1)}, f32[16,8,256]{2,1,0:T(8,128)}, u32[]{:S(2)}) %copy-start.2) | copy-done | bytes 131096
  4.9 0.0 copy-start.3
  4.9 0.8 %copy-done.3 = f32[8,16,128]{2,1,0:T(8,128)S(1)} copy-done((f32[8,16,128]{2,1,0:T(8,128)S(1)}, f32[8,16,128]{2,1,0:T(8,128)}, u32[]{:S(2)}) %copy-start.3) | copy-done | bytes 65560
  5.7 0.0 copy-start.4
  5.7 0.8 %copy-done.4 = f32[8,16,128]{2,1,0:T(8,128)S(1)} copy-done((f32[8,16,128]{2,1,0:T(8,128)S(1)}, f32[8,16,128]{2,1,0:T(8,128)}, u32[]{:S(2)}) %copy-start.4) | copy-done | bytes 65560
  6.6 0.0 copy-start.5
  6.6 0.8 %copy-done.5 = f32[8,16,128]{2,1,0:T(8,128)S(1)} copy-done((f32[8,16,128]{2,1,0:T(8,128)S(1)}, f32[8,16,128]{2,1,0:T(8,128)}, u32[]{:S(2)}) %copy-start.5) | copy-done | bytes 65560
  7.4 34.8 %shard_map.95 = (f32[128,128]{1,0:T(8,128)S(1)}, f32[16,8,256]{2,1,0:T(8,128)S(1)}) custom-call(s32[96]{0:T(128)S(1)} %pad_add_fusion.tables, s32[16]{0:T(128)S(1)} %copy-done.6, f32[128,128]{1,0:T(8,128)S(1)} %bitcast.8, f32[128,128]{1,0:T(8,128)S(1)} %bitcast.9, f32[128,128]{1,0:T(8,128)S(1)} %bitcast.10, f32[16,8,256]{2,1,0:T(8,128)S(1)} %copy-done, ...), custom_call_target="tpu_custom_call" | custom-call | tf_op jit(solution)/shard_map/pallas_call | solution.py:462
  42.2 0.6 %copy.12 = f32[8,16,128]{2,1,0:T(8,128)} copy(f32[8,16,128]{2,1,0:T(8,128)S(1)} %bitcast.11) | data formatting | bytes 131072
  42.8 0.7 %copy.13 = f32[16,8,256]{2,1,0:T(8,128)} copy(f32[16,8,256]{2,1,0:T(8,128)S(1)} %get-tuple-element.13) | data formatting | bytes 262144
  (1 shorter events, 0.0 us)
Async XLA Ops:
  0.6 0.7 %copy-start.6 = (s32[16]{0:T(128)S(1)}, s32[16]{0:T(128)}, u32[]{:S(2)}) copy-start(s32[16]{0:T(128)} %froms.1) | copy-start | bytes 196
  1.3 0.7 %copy-start.7 = (s32[32,2]{0,1:T(2,128)S(1)}, s32[32,2]{0,1:T(2,128)}, u32[]{:S(2)}) copy-start(s32[32,2]{0,1:T(2,128)} %param.14) | copy-start | bytes 772
  2.2 0.9 %copy-start = (f32[16,8,256]{2,1,0:T(8,128)S(1)}, f32[16,8,256]{2,1,0:T(8,128)}, u32[]{:S(2)}) copy-start(f32[16,8,256]{2,1,0:T(8,128)} %prhs_ref.1) | copy-start | bytes 393220
  3.1 0.9 %copy-start.1 = (f32[16,8,256]{2,1,0:T(8,128)S(1)}, f32[16,8,256]{2,1,0:T(8,128)}, u32[]{:S(2)}) copy-start(f32[16,8,256]{2,1,0:T(8,128)} %pcond_ref.1) | copy-start | bytes 393220
  4.0 0.9 %copy-start.2 = (f32[16,8,256]{2,1,0:T(8,128)S(1)}, f32[16,8,256]{2,1,0:T(8,128)}, u32[]{:S(2)}) copy-start(f32[16,8,256]{2,1,0:T(8,128)} %pcap_ref.1) | copy-start | bytes 393220
  4.9 0.8 %copy-start.3 = (f32[8,16,128]{2,1,0:T(8,128)S(1)}, f32[8,16,128]{2,1,0:T(8,128)}, u32[]{:S(2)}) copy-start(f32[8,16,128]{2,1,0:T(8,128)} %param.8) | copy-start | bytes 196612
  5.7 0.8 %copy-start.4 = (f32[8,16,128]{2,1,0:T(8,128)S(1)}, f32[8,16,128]{2,1,0:T(8,128)}, u32[]{:S(2)}) copy-start(f32[8,16,128]{2,1,0:T(8,128)} %param.9) | copy-start | bytes 196612
  6.6 0.8 %copy-start.5 = (f32[8,16,128]{2,1,0:T(8,128)S(1)}, f32[8,16,128]{2,1,0:T(8,128)}, u32[]{:S(2)}) copy-start(f32[8,16,128]{2,1,0:T(8,128)} %param.10) | copy-start | bytes 196612
where the time goes:
time: 43.8 us; the launch traced here: 43.5 us
  Pallas kernels  34.8 us (79%)
  local copies, waits for them, and re-layouts  7.76 us (18%)
  between operations  0.66 us (2%)
    pallas_call x1, Pallas kernels, body(): pl.pallas_call(functools.partial(kernel, n_gx, n_gy, cap_rows), out_shape...  34.8 us
    unnamed x18, local copies, waits for them, and re-layouts  7.76 us

commit v1 on v0

--- a/solution.py
+++ b/solution.py
@@ -122,10 +122,11 @@
 
 
 def kernel(
-    n_gx, n_gy, cap_rows, tables, froms,
-    rhs_ref, cond_ref, capb_ref, prhs_ref, pcond_ref, pcap_ref,
+    n_gx, n_gy, cap_rows, boxes_hbm, froms_hbm,
+    rhs_hbm, cond_hbm, capb_hbm, prhs_hbm, pcond_hbm, pcap_hbm,
     field_ref, patch_ref,
-    tile, side, from_rows, from_side, from_corner,
+    boxes, froms, lists, routes, cond_ref, capb_ref, rhs_ref, pcond_ref, pcap_ref, prhs_ref,
+    load_sem, tile, side, from_rows, from_side, from_corner,
     slots, out1, in1, out2, in2, out3, in3, win1, win2, rest,
     coarse_k, coarse_g, column,
     send_a, recv_a, send_x, recv_x, send_k, recv_k, send_g, recv_g,
@@ -143,6 +144,16 @@
         else:
             pl.when(cond)(action)
 
+    loads = [
+        pltpu.make_async_copy(src, dst, load_sem.at[i])
+        for i, (src, dst) in enumerate((
+            (cond_hbm, cond_ref), (capb_hbm, capb_ref), (rhs_hbm, rhs_ref), (boxes_hbm, boxes),
+            (froms_hbm, froms), (pcond_hbm, pcond_ref), (pcap_hbm, pcap_ref), (prhs_hbm, prhs_ref),
+        ))
+    ]
+    for load in loads:
+        load.start()
+
     barrier = pltpu.get_barrier_semaphore()
 
     def greet(x, y):
@@ -158,6 +169,7 @@
     lane = lax.broadcasted_iota(jnp.int32, (8, 128), 1)
     own = []
     for index, ref in enumerate((cond_ref, capb_ref, rhs_ref)):
+        loads[index].wait()
         rows = [ref[pl.ds(x, 8, stride=16), :] for x in range(16)]
         for x in range(16):
             tile[index, x] = rows[x]
@@ -271,6 +283,25 @@
         start_wait(sends)
         return sends, recvs
 
+    loads[3].wait()
+    loads[4].wait()
+    list_lane = lax.broadcasted_iota(jnp.int32, (1, 128), 1)
+    by_row = jnp.zeros((1, 128), jnp.int32)
+    by_slot = jnp.full((1, 128), -1, jnp.int32)
+    by_from = jnp.zeros((1, 128), jnp.int32)
+    for k in range(32):
+        slot, row = boxes[0, k], boxes[1, k]
+        by_row = jnp.where(list_lane == row, slot, by_row)
+        by_slot = jnp.where(list_lane == slot, row, by_slot)
+    for j in range(16):
+        by_from = jnp.where(list_lane == froms[j], j, by_from)
+    lists[0:1] = by_row
+    lists[1:2] = by_slot
+    lists[2:3] = by_from
+    lists[3:8] = jnp.zeros((5, 128), jnp.int32)
+    route = pltpu.make_async_copy(lists, routes, load_sem.at[8])
+    route.start()
+
     to_half = table(128, 128, lambda s, d: jnp.where(s // 2 == d % 64, 0.25, 0.0))
     rim_map = table(128, 256, lambda s, d: (
         jnp.where((d < 16) & (s == 64 + d // 2), 1.0, 0.0)
@@ -288,6 +319,8 @@
     coarse_k[1, a, 0] = packed_coarse(own[0])
     coarse_k[1, a, 1] = packed_coarse(own[1])
 
+    for load in loads[5:]:
+        load.wait()
     pcond = pcond_ref[...]
     plane = lax.broadcasted_iota(jnp.int32, pcond.shape, 2)
     player = lax.broadcasted_iota(jnp.int32, pcond.shape, 1)
@@ -310,6 +343,8 @@
             + p_north * lanes(values, -1) + lanes(p_north * values, 1)
             + p_above * layers(values, -1) + layers(p_above * values, 1)
         )
+
+    route.wait()
 
     wait_recv(halo_recv)
     count = 16 + 2 * HALO
@@ -341,7 +376,7 @@
 
     windows_into(u_a, slots)
     for r in range(32):
-        out1[r] = slots[tables[r]]
+        out1[r] = slots[routes[0, r]]
     sends1, recvs1 = all_to_all(0, out1, in1)
     sends_k, recvs_k = gather(coarse_k, send_k, recv_k)
     r_0 = residual_of(u_a, source0, stencil0)[HALO:HALO + 16, :, :128]
@@ -357,7 +392,7 @@
     v_a = (1.0 - RELAX) * v_a + p_gain * (p_source + p_around(v_a))
     rest[...] = apply_table(p_source - p_diag * v_a + p_around(v_a), restrict_map)
     for r in range(32):
-        out2[r] = rest[tables[64 + r]]
+        out2[r] = rest[routes[2, r]]
     sends2, recvs2 = all_to_all(1, out2, in2)
 
     wait_recv(recvs_k)
@@ -399,7 +434,7 @@
     for band in range(2):
         items = []
         for col in range(16):
-            at = tables[32 + 16 * band + col]
+            at = routes[1, 16 * band + col]
             flag = jnp.where(at >= 0, 1.0, 0.0).astype(F32)
             items.append(jnp.where(lane // 8 == 8, flag, in2[jnp.maximum(at, 0)]))
         placed = exchange_groups(items)
@@ -427,7 +462,7 @@
 
     windows_into(solved, slots)
     for r in range(32):
-        out3[r] = slots[tables[r]]
+        out3[r] = slots[routes[0, r]]
     sends3, recvs3 = all_to_all(2, out3, in3)
     for x in range(16):
         field_ref[pl.ds(x, 8, stride=16), :] = solved[HALO + x, :, :128]
@@ -445,18 +480,9 @@
 
 
 def body(n_gx, n_gy, rhs_base, cond_base, cap_base, patch_rhs, patch_cond, patch_cap, box_list, patch_from):
-    rows_all = 2 * patch_rhs.shape[0]
-    cap_rows = rows_all // n_gy
-    ids = lax.broadcasted_iota(jnp.int32, (rows_all, 1), 0)
-    slot_ids, send_rows = box_list[:, 0][None, :], box_list[:, 1][None, :]
-    owned = lax.broadcasted_iota(jnp.int32, (1, patch_from.shape[0]), 1)
-    tables = jnp.concatenate([
-        jnp.max(jnp.where(send_rows == ids, slot_ids, 0), axis=1),
-        jnp.max(jnp.where(slot_ids == ids, send_rows, -1), axis=1),
-        jnp.max(jnp.where(patch_from[None, :] == ids, owned, 0), axis=1),
-    ])
+    cap_rows = 2 * patch_rhs.shape[0] // n_gy
     vmem = pl.BlockSpec(memory_space=pltpu.VMEM)
-    smem = pl.BlockSpec(memory_space=pltpu.SMEM)
+    far = pl.BlockSpec(memory_space=pltpu.HBM)
     dma = pltpu.SemaphoreType.DMA
     buffer = pltpu.VMEM((32, 8, 128), F32)
     field, patches = pl.pallas_call(
@@ -465,9 +491,14 @@
             jax.ShapeDtypeStruct((128, 128), F32),
             jax.ShapeDtypeStruct(patch_rhs.shape, F32),
         ),
-        in_specs=[smem, smem] + [vmem] * 6,
+        in_specs=[far] * 8,
         out_specs=(vmem, vmem),
         scratch_shapes=[
+            pltpu.SMEM((2, 32), jnp.int32), pltpu.SMEM((16,), jnp.int32),
+            pltpu.VMEM((8, 128), jnp.int32), pltpu.SMEM((8, 128), jnp.int32),
+            pltpu.VMEM((128, 128), F32), pltpu.VMEM((128, 128), F32), pltpu.VMEM((128, 128), F32),
+            pltpu.VMEM(patch_rhs.shape, F32), pltpu.VMEM(patch_rhs.shape, F32),
+            pltpu.VMEM(patch_rhs.shape, F32), dma((9,)),
             pltpu.VMEM((3, 16, 8, 128), F32),
             pltpu.VMEM((2, 3, 8, 128), F32),
             pltpu.VMEM((2, 3, HALO, 8, 128), F32),
@@ -486,10 +517,10 @@
             dma((3, n_gx)), dma((3, n_gx)),
         ],
         compiler_params=pltpu.CompilerParams(
-            collective_id=0, has_side_effects=True, vmem_limit_bytes=48 * 1024 * 1024
+            collective_id=0, has_side_effects=True, vmem_limit_bytes=64 * 1024 * 1024
         ),
     )(
-        tables, patch_from,
+        box_list.T, patch_from,
         rhs_base.reshape(128, 128), cond_base.reshape(128, 128), cap_base.reshape(128, 128),
         patch_rhs, patch_cond, patch_cap,
     )

time: 43.8 us -> 38 us (0.87)
  local copies, waits for them, and re-layouts: 7.76 us -> 2.17 us
    unnamed x18 -> x4, local copies, waits for them, and re-layouts: 7.76 us -> 2.17 us
where the time goes in v1:
time: 38 us; the launch traced here: 37.8 us
  Pallas kernels  35 us (92%)
  local copies, waits for them, and re-layouts  2.17 us (6%)
  between operations  0.65 us (2%)
    pallas_call x1, Pallas kernels, body(): pl.pallas_call(functools.partial(kernel, n_gx, n_gy, cap_rows), out_shape...  35 us
    unnamed x4, local copies, waits for them, and re-layouts  2.17 us

profile of v1, /device:TPU:0, one launch (start us, length us, event | category | flops | bytes accessed | tf_op | source)
XLA Modules:
  0.0 37.8 jit_solution(12045018599324161286)
XLA Ops:
  0.6 35.0 %shard_map.95 = (f32[128,128]{1,0:T(8,128)}, f32[16,8,256]{2,1,0:T(8,128)}) custom-call(s32[2,32]{1,0:T(2,128)} %bitcast.9, s32[16]{0:T(128)} %froms_hbm.1, f32[128,128]{1,0:T(8,128)} %bitcast.6, f32[128,128]{1,0:T(8,128)} %bitcast.7, f32[128,128]{1,0:T(8,128)} %bitcast.8, f32[16,8,256]{2,1,0:T(8,128)} %prhs_hbm.1, f32[16,8,256]{2,1,0:T(8,128)} %pcond_hbm.1, ...), custom_call_target="tpu_custom_call" | custom-call | tf_op jit(solution)/shard_map/pallas_call | solution.py:488
  35.7 0.0 copy-start
  35.7 1.5 %copy.12 = f32[8,16,128]{2,1,0:T(8,128)} copy(f32[8,16,128]{2,1,0:T(8,128)} %bitcast.5) | data formatting | bytes 131072
  37.2 0.0 copy-done
  37.2 0.7 %copy.13 = f32[16,8,256]{2,1,0:T(8,128)} copy(f32[16,8,256]{2,1,0:T(8,128)S(1)} %copy-done) | data formatting | bytes 262144
Async XLA Ops:
  35.7 1.5 %copy-start = (f32[16,8,256]{2,1,0:T(8,128)S(1)}, f32[16,8,256]{2,1,0:T(8,128)}, u32[]{:S(2)}) copy-start(f32[16,8,256]{2,1,0:T(8,128)} %get-tuple-element.9) | copy-start | bytes 393220

commit v2 on v1

--- a/solution.py
+++ b/solution.py
@@ -237,25 +237,25 @@
             halo_recv.append((cond, arrive))
     start_wait(halo_send)
 
-    def all_to_all(phase, src, dst):
+    def all_to_all(phase, src, dst, rows):
         sends, recvs = [], []
         for d in range(1, n_gy):
             def out(d=d):
                 to = lax.rem(b + d, n_gy)
                 return remote(
-                    src.at[pl.ds(to * cap_rows, cap_rows)], dst.at[pl.ds(b * cap_rows, cap_rows)],
+                    src.at[pl.ds(to * rows, rows)], dst.at[pl.ds(b * rows, rows)],
                     send_x.at[phase, d], recv_x.at[phase, d], a, to,
                 )
 
             def arrive(d=d):
                 at = lax.rem(b + n_gy - d, n_gy)
-                piece = dst.at[pl.ds(at * cap_rows, cap_rows)]
+                piece = dst.at[pl.ds(at * rows, rows)]
                 return remote(piece, piece, send_x.at[phase, d], recv_x.at[phase, d], a, at)
 
             sends.append((None, out))
             recvs.append((None, arrive))
         start_wait(sends)
-        mine = pl.ds(b * cap_rows, cap_rows)
+        mine = pl.ds(b * rows, rows)
         dst[mine] = src[mine]
         return sends, recvs
 
@@ -309,7 +309,7 @@
         + jnp.where((d % 16 == 0) & (s == 80 + d // 32), 1.0, 0.0)
         + jnp.where((d % 16 == 15) & (s == 88 + d // 32), 1.0, 0.0)
     ))
-    restrict_map = table(256, 128, lambda s, d: jnp.where(s // 32 * 8 + s % 16 // 2 == d, 0.25, 0.0))
+    restrict_map = table(256, 128, lambda s, d: jnp.where(s // 32 * 8 + s % 16 // 2 == d % 64, 0.25, 0.0))
 
     def packed_coarse(values):
         halves = apply_table(pair_rows(values), to_half)
@@ -377,7 +377,7 @@
     windows_into(u_a, slots)
     for r in range(32):
         out1[r] = slots[routes[0, r]]
-    sends1, recvs1 = all_to_all(0, out1, in1)
+    sends1, recvs1 = all_to_all(0, out1, in1, cap_rows)
     sends_k, recvs_k = gather(coarse_k, send_k, recv_k)
     r_0 = residual_of(u_a, source0, stencil0)[HALO:HALO + 16, :, :128]
 
@@ -391,9 +391,13 @@
     v_a = p_gain * p_source
     v_a = (1.0 - RELAX) * v_a + p_gain * (p_source + p_around(v_a))
     rest[...] = apply_table(p_source - p_diag * v_a + p_around(v_a), restrict_map)
-    for r in range(32):
-        out2[r] = rest[routes[2, r]]
-    sends2, recvs2 = all_to_all(1, out2, in2)
+    pack = 2 if cap_rows % 2 == 0 else 1
+    for r in range(0, 32, pack):
+        if pack == 2:
+            out2[r // 2] = jnp.where(lane < 64, rest[routes[2, r]], rest[routes[2, r + 1]])
+        else:
+            out2[r] = rest[routes[2, r]]
+    sends2, recvs2 = all_to_all(1, out2, in2, cap_rows // pack)
 
     wait_recv(recvs_k)
     rows1 = 8 * n_gx
@@ -436,7 +440,11 @@
         for col in range(16):
             at = routes[1, 16 * band + col]
             flag = jnp.where(at >= 0, 1.0, 0.0).astype(F32)
-            items.append(jnp.where(lane // 8 == 8, flag, in2[jnp.maximum(at, 0)]))
+            row = jnp.maximum(at, 0)
+            item = in2[row // pack]
+            if pack == 2:
+                item = jnp.where(lane >= 128 * (1 - row % 2), lanes(item, 64), item)
+            items.append(jnp.where(lane // 8 == 8, flag, item))
         placed = exchange_groups(items)
         for i in range(8):
             pieces.append(jnp.where(placed[8] > 0.5, placed[i], r_0[8 * band + i]))
@@ -463,7 +471,7 @@
     windows_into(solved, slots)
     for r in range(32):
         out3[r] = slots[routes[0, r]]
-    sends3, recvs3 = all_to_all(2, out3, in3)
+    sends3, recvs3 = all_to_all(2, out3, in3, cap_rows)
     for x in range(16):
         field_ref[pl.ds(x, 8, stride=16), :] = solved[HALO + x, :, :128]
     grow_map = table(128, 256, lambda s, d: jnp.where(s == d // 32 * 8 + d % 16 // 2, 1.0, 0.0))

time: 38 us -> 37.5 us (0.987)
  Pallas kernels: 35 us -> 34.6 us
    pallas_call x1, Pallas kernels: 35 us -> 34.6 us  [body(): pl.pallas_call(functools.partial(kernel, n_gx, n_gy, cap_rows), out_shape...]
where the time goes in v2:
time: 37.5 us; the launch traced here: 37.4 us
  Pallas kernels  34.6 us (92%)
  local copies, waits for them, and re-layouts  2.17 us (6%)
  between operations  0.65 us (2%)
    pallas_call x1, Pallas kernels, body(): pl.pallas_call(functools.partial(kernel, n_gx, n_gy, cap_rows), out_shape...  34.6 us
    unnamed x4, local copies, waits for them, and re-layouts  2.17 us

profile of v2, /device:TPU:0, one launch (start us, length us, event | category | flops | bytes accessed | tf_op | source)
XLA Modules:
  0.0 37.4 jit_solution(14053784029044324896)
XLA Ops:
  0.6 34.6 %shard_map.95 = (f32[128,128]{1,0:T(8,128)}, f32[16,8,256]{2,1,0:T(8,128)}) custom-call(s32[2,32]{1,0:T(2,128)} %bitcast.9, s32[16]{0:T(128)} %froms_hbm.1, f32[128,128]{1,0:T(8,128)} %bitcast.6, f32[128,128]{1,0:T(8,128)} %bitcast.7, f32[128,128]{1,0:T(8,128)} %bitcast.8, f32[16,8,256]{2,1,0:T(8,128)} %prhs_hbm.1, f32[16,8,256]{2,1,0:T(8,128)} %pcond_hbm.1, ...), custom_call_target="tpu_custom_call" | custom-call | tf_op jit(solution)/shard_map/pallas_call | solution.py:496
  35.2 0.0 copy-start
  35.2 1.5 %copy.12 = f32[8,16,128]{2,1,0:T(8,128)} copy(f32[8,16,128]{2,1,0:T(8,128)} %bitcast.5) | data formatting | bytes 131072
  36.7 0.0 copy-done
  36.7 0.7 %copy.13 = f32[16,8,256]{2,1,0:T(8,128)} copy(f32[16,8,256]{2,1,0:T(8,128)S(1)} %copy-done) | data formatting | bytes 262144
Async XLA Ops:
  35.2 1.5 %copy-start = (f32[16,8,256]{2,1,0:T(8,128)S(1)}, f32[16,8,256]{2,1,0:T(8,128)}, u32[]{:S(2)}) copy-start(f32[16,8,256]{2,1,0:T(8,128)} %get-tuple-element.9) | copy-start | bytes 393220
